TPU v7x, 128 devices: a whole 4x4x4 slice. The times are simulated.
128 devices in a mesh: scen: 16 (over y, x), base: 8 (over z, core).
Axes of the slice: x: 4, y: 4, z: 4, core: 2. Of those that a mesh axis runs over, the one named last changes fastest.
Arguments:
- right_sides: float32 [32, 8192], P(None, 'scen'), may hold values from -6 to 6
- base_hessian: float32 [8192], P('scen'), may hold values from 0.05 to 1
- sensitivity: float32 [32, 8192, 128], P('base', 'scen'), may hold values from -0.125 to 0.125
- weights: float32 [32, 128], P('base'), may hold values from 0.1 to 10
- outage_factors: float32 [32, 128], P('base'), may hold values from -1 to 1
- outaged: int32 [32], P('base'), may hold values from 0 to 127
Outputs:
- step: float32 [32, 8192], P(None, 'scen')
- flow_step: float32 [32, 32, 128], P('base')
All inputs are finite; a program needn't handle non-finite values.
Results may differ from a plain program's by a relative error of at most 0.0003.
Values sent between devices are 32-bit elements; how exact they have to be, the bound alone decides.
A program may use at most 64 MiB of HBM per device.

v0:
```python
import jax
import jax.numpy as jnp
from jax import lax
from jax.sharding import PartitionSpec as P

ITERS = 5


HIGHEST_PREC = lax.Precision.HIGHEST


def sent_to_all(value, axis):
    count = lax.axis_size(axis)
    return lax.all_to_all(
        jnp.broadcast_to(value[None], (count, *value.shape)), axis, 0, 0, tiled=True
    )


def taken_together(value, axis):
    return sent_to_all(value, axis).sum(axis=0)


def packed_total(arrays, axis):
    ends = [0]
    for a in arrays:
        ends.append(ends[-1] + a.size)
    total = taken_together(jnp.concatenate([a.ravel() for a in arrays]), axis)
    return tuple((total[b:e].reshape(a.shape) for a, b, e in zip(arrays, ends, ends[1:])))


def contingency_terms(flows_sum, weights, selector, factors):
    outaged_flow = jnp.sum(flows_sum * selector[:, None, :], axis=2, keepdims=True)
    post_flows = flows_sum + factors[:, None, :] * outaged_flow
    weighted = weights[:, None, :] * post_flows
    outaged_sum = jnp.sum(factors[:, None, :] * weighted, axis=2, keepdims=True)
    spread_back = weighted + selector[:, None, :] * outaged_sum
    return (post_flows, weighted, spread_back)


def per_device(right_sides, base_hessian, sensitivity, weights, outage_factors, outaged):
    chosen = lax.broadcasted_iota(jnp.int32, weights.shape, 1) == outaged[:, None]
    selector = chosen.astype(jnp.float32)
    factors = jnp.where(chosen, -1.0, outage_factors)

    def squares(vector):
        return taken_together(jnp.sum(vector * vector, axis=1), "scen")

    residual = right_sides
    direction_share = residual
    direction_full = right_sides
    solution = jnp.zeros_like(residual)
    norm_now = squares(residual)
    for iteration in range(ITERS):
        apply_partial_value = jnp.einsum(
            "knm,rn->krm", sensitivity, direction_full, precision=HIGHEST_PREC
        )
        base_term = jnp.sum(base_hessian[None, :] * direction_full * direction_full, axis=1)
        apply_flows_sum, base_curv = packed_total((apply_partial_value, base_term), "scen")
        apply_post_flows, apply_weighted, apply_spread_back = contingency_terms(
            apply_flows_sum, weights, selector, factors
        )
        partial_image = jnp.einsum(
            "knm,krm->rn", sensitivity, apply_spread_back, precision=HIGHEST_PREC
        )
        contingent_term = jnp.sum(apply_post_flows * apply_weighted, axis=(0, 2))
        product, contingent = packed_total((partial_image, contingent_term), "base")
        product = product + base_hessian[None, :] * direction_full
        curvature = base_curv + contingent
        product, curvature = (product, curvature)
        step_len = norm_now / curvature
        solution = solution + step_len[:, None] * direction_share
        residual = residual - step_len[:, None] * product
        if iteration + 1 < ITERS:
            norm_next = squares(residual)
            direction_share = residual + (norm_next / norm_now)[:, None] * direction_share
            direction_full = direction_share
            norm_now = norm_next
    partial_value = jnp.einsum("knm,rn->krm", sensitivity, solution, precision=HIGHEST_PREC)
    flows_sum = taken_together(partial_value, "scen")
    post_flows, weighted, spread_back = contingency_terms(flows_sum, weights, selector, factors)
    return (solution, weighted)


def solution(mesh):
    placed = (
        P(None, "scen"),
        P("scen"),
        P("base", "scen", None),
        P("base", None),
        P("base", None),
        P("base"),
    )
    return jax.shard_map(
        per_device,
        mesh=mesh,
        in_specs=placed,
        out_specs=(P(None, "scen"), P("base", None, None)),
        check_vma=False,
    )
```

profile of v0, /device:TPU:1, one launch (start us, length us, event | category | flops | bytes accessed | tf_op | source)
XLA Modules:
  0.0 271.8 jit_solution(3446775721235983716)
XLA Ops:
  0.6 1.0 multiply_reduce_fusion.4
  1.9 1.5 fusion.51
  3.5 1.5 broadcast_in_dim.37
  5.0 7.7 %all-to-all-start.1 = ((f32[16,1,16416]{2,1,0:T(1,128)}), f32[16,1,16416]{2,1,0:T(1,128)S(1)}, u32[]{:S(2)}, u32[]{:S(2)}) async-start(f32[16,1,16416]{2,1,0:T(1,128)} %broadcast_in_dim.37), calls=%async_computation.1 | async-start | bytes 2113536 | tf_op jit(solution)/shard_map/all_to_all | solution.py:14
  12.9 15.9 %all-to-all-done.1 = f32[16,1,16416]{2,1,0:T(1,128)S(1)} async-done(((f32[16,1,16416]{2,1,0:T(1,128)}), f32[16,1,16416]{2,1,0:T(1,128)S(1)}, u32[]{:S(2)}, u32[]{:S(2)}) %all-to-all-start.1) | async-done | bytes 1050656 | tf_op jit(solution)/shard_map/all_to_all | solution.py:14
  28.8 0.6 broadcast_in_dim.36
  29.4 4.2 %all-to-all-start = ((f32[16,1,32]{2,1,0:T(1,128)}), f32[16,1,32]{2,1,0:T(1,128)S(1)}, u32[]{:S(2)}, u32[]{:S(2)}) async-start(f32[16,1,32]{2,1,0:T(1,128)} %broadcast_in_dim.36), calls=%async_computation | async-start | bytes 16384 | tf_op jit(solution)/shard_map/all_to_all | solution.py:14
  33.6 0.7 reduce_sum.381
  34.3 0.8 fusion.19
  35.1 1.1 convolution_bitcast_fusion.5
  36.2 3.7 %all-to-all-done = f32[16,1,32]{2,1,0:T(1,128)S(1)} async-done(((f32[16,1,32]{2,1,0:T(1,128)}), f32[16,1,32]{2,1,0:T(1,128)S(1)}, u32[]{:S(2)}, u32[]{:S(2)}) %all-to-all-start) | async-done | bytes 2080 | tf_op jit(solution)/shard_map/all_to_all | solution.py:14
  40.0 1.1 broadcast_in_dim.39
  41.0 8.4 %all-to-all-start.2 = ((f32[8,1,16416]{2,1,0:T(1,128)}), f32[8,1,16416]{2,1,0:T(1,128)S(1)}, u32[]{:S(2)}, u32[]{:S(2)}) async-start(f32[8,1,16416]{2,1,0:T(1,128)} %broadcast_in_dim.39), calls=%async_computation.2 | async-start | bytes 1056768 | tf_op jit(solution)/shard_map/all_to_all | solution.py:14
  49.5 9.5 %all-to-all-done.2 = f32[8,1,16416]{2,1,0:T(1,128)S(1)} async-done(((f32[8,1,16416]{2,1,0:T(1,128)}), f32[8,1,16416]{2,1,0:T(1,128)S(1)}, u32[]{:S(2)}, u32[]{:S(2)}) %all-to-all-start.2) | async-done | bytes 525344 | tf_op jit(solution)/shard_map/all_to_all | solution.py:14
  59.6 9.1 %all_to_all.95 = f32[16,1,32]{2,1,0:T(1,128)S(1)} all-to-all(f32[16,1,32]{2,1,0:T(1,128)S(1)} %broadcast_in_dim.40), channel_id=1, replica_groups=mesh['scen'=16,'base'=8] {'scen'}, dimensions={0} | all-to-all | bytes 4096 | tf_op jit(solution)/shard_map/all_to_all | solution.py:14
  69.0 0.7 fusion.49
  69.8 0.5 broadcast_in_dim.41
  70.3 17.9 %all_to_all.96 = f32[16,1,16416]{2,1,0:T(1,128)S(1)} all-to-all(f32[16,1,16416]{2,1,0:T(1,128)S(1)} %broadcast_in_dim.41), channel_id=1, replica_groups=mesh['scen'=16,'base'=8] {'scen'}, dimensions={0} | all-to-all | bytes 2101248 | tf_op jit(solution)/shard_map/all_to_all | solution.py:14
  88.2 0.7 reduce_sum.389
  88.8 0.8 fusion.21
  89.6 1.1 convolution_bitcast_fusion.4
  91.0 15.8 %all_to_all.97 = f32[8,1,16416]{2,1,0:T(1,128)S(1)} all-to-all(f32[8,1,16416]{2,1,0:T(1,128)S(1)} %broadcast_in_dim.42), channel_id=1, replica_groups=mesh['scen'=16,'base'=8] {'base'}, dimensions={0} | all-to-all | bytes 1050624 | tf_op jit(solution)/shard_map/all_to_all | solution.py:14
  107.4 9.1 %all_to_all.98 = f32[16,1,32]{2,1,0:T(1,128)S(1)} all-to-all(f32[16,1,32]{2,1,0:T(1,128)S(1)} %broadcast_in_dim.43), channel_id=1, replica_groups=mesh['scen'=16,'base'=8] {'scen'}, dimensions={0} | all-to-all | bytes 4096 | tf_op jit(solution)/shard_map/all_to_all | solution.py:14
  116.8 0.7 fusion.47
  117.5 0.5 broadcast_in_dim.44
  118.1 18.8 %all_to_all.99 = f32[16,1,16416]{2,1,0:T(1,128)S(1)} all-to-all(f32[16,1,16416]{2,1,0:T(1,128)S(1)} %broadcast_in_dim.44), channel_id=1, replica_groups=mesh['scen'=16,'base'=8] {'scen'}, dimensions={0} | all-to-all | bytes 2101248 | tf_op jit(solution)/shard_map/all_to_all | solution.py:14
  136.9 0.7 reduce_sum.397
  137.6 0.8 fusion.23
  138.4 1.1 convolution_bitcast_fusion.3
  139.8 15.1 %all_to_all.100 = f32[8,1,16416]{2,1,0:T(1,128)S(1)} all-to-all(f32[8,1,16416]{2,1,0:T(1,128)S(1)} %broadcast_in_dim.45), channel_id=1, replica_groups=mesh['scen'=16,'base'=8] {'base'}, dimensions={0} | all-to-all | bytes 1050624 | tf_op jit(solution)/shard_map/all_to_all | solution.py:14
  155.5 9.1 %all_to_all.101 = f32[16,1,32]{2,1,0:T(1,128)S(1)} all-to-all(f32[16,1,32]{2,1,0:T(1,128)S(1)} %broadcast_in_dim.46), channel_id=1, replica_groups=mesh['scen'=16,'base'=8] {'scen'}, dimensions={0} | all-to-all | bytes 4096 | tf_op jit(solution)/shard_map/all_to_all | solution.py:14
  164.8 0.7 fusion.45
  165.5 0.5 broadcast_in_dim.47
  166.1 18.8 %all_to_all.102 = f32[16,1,16416]{2,1,0:T(1,128)S(1)} all-to-all(f32[16,1,16416]{2,1,0:T(1,128)S(1)} %broadcast_in_dim.47), channel_id=1, replica_groups=mesh['scen'=16,'base'=8] {'scen'}, dimensions={0} | all-to-all | bytes 2101248 | tf_op jit(solution)/shard_map/all_to_all | solution.py:14
  184.9 0.7 reduce_sum.405
  185.5 0.8 fusion.25
  186.3 1.1 convolution_bitcast_fusion.2
  187.7 15.1 %all_to_all.103 = f32[8,1,16416]{2,1,0:T(1,128)S(1)} all-to-all(f32[8,1,16416]{2,1,0:T(1,128)S(1)} %broadcast_in_dim.48), channel_id=1, replica_groups=mesh['scen'=16,'base'=8] {'base'}, dimensions={0} | all-to-all | bytes 1050624 | tf_op jit(solution)/shard_map/all_to_all | solution.py:14
  203.5 9.0 %all_to_all.104 = f32[16,1,32]{2,1,0:T(1,128)S(1)} all-to-all(f32[16,1,32]{2,1,0:T(1,128)S(1)} %broadcast_in_dim.49), channel_id=1, replica_groups=mesh['scen'=16,'base'=8] {'scen'}, dimensions={0} | all-to-all | bytes 4096 | tf_op jit(solution)/shard_map/all_to_all | solution.py:14
  212.7 0.7 fusion.43
  214.0 18.8 %all_to_all.105 = f32[16,1,16416]{2,1,0:T(1,128)S(1)} all-to-all(f32[16,1,16416]{2,1,0:T(1,128)S(1)} %broadcast_in_dim.50), channel_id=1, replica_groups=mesh['scen'=16,'base'=8] {'scen'}, dimensions={0} | all-to-all | bytes 2101248 | tf_op jit(solution)/shard_map/all_to_all | solution.py:14
  232.8 0.7 reduce_sum.413
  233.5 0.8 fusion.27
  234.3 1.1 convolution_bitcast_fusion.1
  235.7 15.1 %all_to_all.106 = f32[8,1,16416]{2,1,0:T(1,128)S(1)} all-to-all(f32[8,1,16416]{2,1,0:T(1,128)S(1)} %broadcast_in_dim.51), channel_id=1, replica_groups=mesh['scen'=16,'base'=8] {'base'}, dimensions={0} | all-to-all | bytes 1050624 | tf_op jit(solution)/shard_map/all_to_all | solution.py:14
  251.3 0.7 convolution_bitcast_fusion
  252.2 18.8 %all_to_all.107 = f32[16,4,32,128]{3,2,1,0:T(8,128)S(1)} all-to-all(f32[16,4,32,128]{3,2,1,0:T(8,128)S(1)} %broadcast_in_dim.52), channel_id=1, replica_groups=mesh['scen'=16,'base'=8] {'scen'}, dimensions={0} | all-to-all | bytes 2097152 | tf_op jit(solution)/shard_map/all_to_all | solution.py:14
  271.1 0.7 fusion.18
  (83 shorter events, 6.3 us)
Async XLA Ops:
  0.6 1.3 copy-start
  5.0 7.7 %copy-start.5 = (s32[4]{0:T(128)S(1)}, s32[4]{0:T(128)}, u32[]{:S(2)}) copy-start(s32[4]{0:T(128)} %param.11) | copy-start | bytes 52
  5.0 7.8 %copy-start.6 = (f32[4,128]{1,0:T(4,128)S(1)}, f32[4,128]{1,0:T(4,128)}, u32[]{:S(2)}) copy-start(f32[4,128]{1,0:T(4,128)} %param.10) | copy-start | bytes 6148
  5.0 23.8 %all-to-all-start.1 = ((f32[16,1,16416]{2,1,0:T(1,128)}), f32[16,1,16416]{2,1,0:T(1,128)S(1)}, u32[]{:S(2)}, u32[]{:S(2)}) async-start(f32[16,1,16416]{2,1,0:T(1,128)} %broadcast_in_dim.37), calls=%async_computation.1 | async-start | bytes 2113536 | tf_op jit(solution)/shard_map/all_to_all | solution.py:14
  12.7 21.6 %copy-start.4 = (f32[4,128]{1,0:T(4,128)S(1)}, f32[4,128]{1,0:T(4,128)}, u32[]{:S(2)}) copy-start(f32[4,128]{1,0:T(4,128)} %param.9) | copy-start | bytes 6148
  29.4 10.5 %all-to-all-start = ((f32[16,1,32]{2,1,0:T(1,128)}), f32[16,1,32]{2,1,0:T(1,128)S(1)}, u32[]{:S(2)}, u32[]{:S(2)}) async-start(f32[16,1,32]{2,1,0:T(1,128)} %broadcast_in_dim.36), calls=%async_computation | async-start | bytes 16384 | tf_op jit(solution)/shard_map/all_to_all | solution.py:14
  41.0 18.4 %copy-start.1 = (f32[32,512]{1,0:T(8,128)S(1)}, f32[32,512]{1,0:T(8,128)}, u32[]{:S(2)}) copy-start(f32[32,512]{1,0:T(8,128)} %param.6) | copy-start | bytes 196612
  41.0 18.4 %copy-start.3 = (f32[512]{0:T(512)S(1)}, f32[512]{0:T(512)}, u32[]{:S(2)}) copy-start(f32[512]{0:T(512)} %param.7) | copy-start | bytes 6148
  41.0 17.9 %all-to-all-start.2 = ((f32[8,1,16416]{2,1,0:T(1,128)}), f32[8,1,16416]{2,1,0:T(1,128)S(1)}, u32[]{:S(2)}, u32[]{:S(2)}) async-start(f32[8,1,16416]{2,1,0:T(1,128)} %broadcast_in_dim.39), calls=%async_computation.2 | async-start | bytes 1056768 | tf_op jit(solution)/shard_map/all_to_all | solution.py:14
  251.3 0.9 copy-start.2
where the time goes:
time: 273 us; the launch traced here: 272 us
  blocking collectives  191 us (70%)
  waiting for transfers between devices  29.1 us (11%)
  starting transfers between devices  20.3 us (7%)
  other arithmetic  13 us (5%)
  matrix products  10.5 us (4%)
  local copies, waits for them, and re-layouts  7.08 us (3%)
    all_to_all x13, blocking collectives, sent_to_all(): lax.all_to_all(jnp.broadcast_to(value[None], (count, *value.shape)), axis...  191 us
    all_to_all x3, waiting for transfers between devices, sent_to_all(): lax.all_to_all(jnp.broadcast_to(value[None], (count, *value.shape)), axis...  29.1 us
    all_to_all x3, starting transfers between devices, sent_to_all(): lax.all_to_all(jnp.broadcast_to(value[None], (count, *value.shape)), axis...  20.3 us
    broadcast_in_dim x16, local copies, waits for them, and re-layouts, sent_to_all(): jnp.broadcast_to(value[None], (count, *value.shape))  6.63 us
  transfers between devices with their start and end apart: 3, of which 3 were waited for; matrix products, arithmetic and copies ran while one was open for 1% of the time, Pallas kernels for 0%

commit v1 on v0

v1 whole, which is shorter than its diff:
```python
import functools

import jax
import jax.numpy as jnp
from jax import lax
from jax.experimental import pallas as pl
from jax.experimental.pallas import tpu as pltpu
from jax.sharding import PartitionSpec as P

ITERS = 5
MESH = pl.DeviceIdType.MESH
F32 = jnp.float32
BF16 = jnp.bfloat16


def halves(value):
    high = value.astype(BF16)
    return high, (value - high.astype(F32)).astype(BF16)


def kernel(S, B, b_ref, h_ref, a_ref, w_ref, f_ref, o_ref, x_ref, y_ref,
           c_hi, c_lo, lhs, flow_out, flow_in, total, image_out, image_in, resid,
           p_ref, w_own, gp_ref, gs_ref, send, recv):
    K, N, M = a_ref.shape
    R = b_ref.shape[0]
    Q = R // 8
    H = B // Q
    W = N // H
    s = lax.axis_index("scen")
    b = lax.axis_index("base")

    barrier = pltpu.get_barrier_semaphore()
    for d in range(1, S):
        pl.semaphore_signal(barrier, inc=1, device_id=(lax.rem(s + d, S), b), device_id_type=MESH)
    for d in range(1, B):
        pl.semaphore_signal(barrier, inc=1, device_id=(s, lax.rem(b + d, B)), device_id_type=MESH)

    lane_m = lax.broadcasted_iota(jnp.int32, (1, M), 1)
    for k in range(K):
        chosen = lane_m == o_ref[k]
        root = jnp.sqrt(w_ref[k : k + 1, :])
        factor = jnp.where(chosen, -1.0, f_ref[k : k + 1, :]) * root
        a = a_ref[k]
        at = jnp.sum(jnp.where(chosen, a, 0.0), axis=1, keepdims=True)
        hi, lo = halves(a * root + at * factor)
        c_hi[:, k * M : (k + 1) * M] = hi
        c_lo[:, k * M : (k + 1) * M] = lo

    for q in range(Q):
        for t in range(H):
            resid[0, H * q + t] = b_ref[8 * q : 8 * q + 8, t * W : (t + 1) * W]
    x_ref[...] = jnp.zeros_like(x_ref)
    p_ref[...] = jnp.zeros_like(p_ref)
    w_own[...] = jnp.zeros_like(w_own)
    gp_ref[...] = jnp.zeros_like(gp_ref)
    gs_ref[...] = jnp.zeros_like(gs_ref)

    lane = lax.broadcasted_iota(jnp.int32, (8, 128), 1)
    sub = lax.broadcasted_iota(jnp.int32, (8, 128), 0)

    def row_of(columns, base):
        out = jnp.zeros((8, 128), F32)
        for q in range(Q):
            out = out + jnp.where(lane == sub + (base + 8 * q), columns[q], 0.0)
        return jnp.sum(out, axis=0, keepdims=True)

    def column_of(row, base):
        return jnp.sum(jnp.where(lane == sub + base, row, 0.0), axis=1, keepdims=True)

    def sends(phase, count, axis, src, dst):
        for d in range(1, count):
            if axis == "scen":
                to = lax.rem(s + d, count)
                device = (to, b)
            else:
                to = lax.rem(b + d, count)
                device = (s, to)
            pltpu.make_async_remote_copy(
                src_ref=src(to), dst_ref=dst(to), send_sem=send.at[phase], recv_sem=recv.at[phase],
                device_id=device, device_id_type=MESH,
            ).start()

    def waits(sems, phase, ref):
        pltpu.make_async_copy(ref, ref, sems.at[phase]).wait()

    def flows(now):
        rows = []
        squares, bent = [], []
        for q in range(Q):
            r = jnp.concatenate([resid[now, H * q + t] for t in range(H)], axis=1)
            rows.append(r)
            rr = r * r
            squares.append(jnp.sum(rr, axis=1, keepdims=True))
            bent.append(jnp.sum(rr * h_ref[...], axis=1, keepdims=True))
        hi, lo = halves(jnp.concatenate(rows, axis=0))
        lhs[:R, :] = hi
        lhs[R:, :] = lo
        big = jnp.dot(lhs[...], c_hi[...], preferred_element_type=F32)
        part = big[:R] + big[R:] + jnp.dot(lhs[:R], c_lo[...], preferred_element_type=F32)
        for k in range(K):
            for q in range(Q):
                flow_out[k * Q + q] = part[8 * q : 8 * q + 8, k * M : (k + 1) * M]
        sends(0, S, "scen", lambda to: flow_out.at[to], lambda to: flow_in.at[s])
        flow_in[s] = flow_out[s]
        scalars = row_of(squares, 0) + row_of(bent, R)
        total[s, 8:9, :] = scalars
        waits(recv, 0, flow_in.at[pl.ds(0, S - 1)])
        tile = flow_in[0]
        for t in range(1, S):
            tile = tile + flow_in[t]
        total[s, 0:8, :] = tile
        sends(1, S, "scen", lambda to: total.at[s, pl.ds(0, 9)], lambda to: total.at[s, pl.ds(0, 9)])
        waits(send, 0, flow_out.at[pl.ds(0, S - 1)])
        waits(recv, 1, total.at[pl.ds(0, S - 1), pl.ds(0, 9)])
        waits(send, 1, total.at[pl.ds(0, S - 1), pl.ds(0, 9)])
        row = total[0, 8:9, :]
        for t in range(1, S):
            row = row + total[t, 8:9, :]
        g = [[total[k * Q + q, 0:8, :] for k in range(K)] for q in range(Q)]
        curv = []
        for q in range(Q):
            squared = g[q][0] * g[q][0]
            for k in range(1, K):
                squared = squared + g[q][k] * g[q][k]
            curv.append(jnp.sum(squared, axis=1, keepdims=True))
        return g, row, row_of(curv, 2 * R)

    def coefficients(first, row, rest, gamma_old, alpha_old):
        out = []
        for q in range(Q):
            gamma = column_of(row, 8 * q)
            beta = jnp.where(first, 0.0, gamma / gamma_old[q])
            delta = column_of(rest, 8 * q)
            alpha = gamma / (delta - beta * (gamma / alpha_old[q]))
            out.append((gamma, beta, alpha))
        return out

    def move(now, g, coef):
        for q in range(Q):
            _, beta, alpha = coef[q]
            for t in range(H):
                p = resid[now, H * q + t] + beta * p_ref[H * q + t]
                p_ref[H * q + t] = p
                rows, cols = slice(8 * q, 8 * q + 8), slice(t * W, (t + 1) * W)
                x_ref[rows, cols] = x_ref[rows, cols] + alpha * p
            for k in range(K):
                gp = g[q][k] + beta * gp_ref[k, 8 * q : 8 * q + 8, :]
                gp_ref[k, 8 * q : 8 * q + 8, :] = gp
                gs_ref[k, 8 * q : 8 * q + 8, :] = gs_ref[k, 8 * q : 8 * q + 8, :] + alpha * gp

    pl.semaphore_wait(barrier, S - 1 + B - 1)

    mine_q = b // H
    mine_t = lax.rem(b, H)
    nt = (((1,), (1,)), ((), ()))

    def step(i, carry):
        gamma_old, alpha_old = carry
        now, later = lax.rem(i, 2), lax.rem(i + 1, 2)
        g, row, curv = flows(now)
        hi, lo = halves(jnp.concatenate([jnp.concatenate(g[q], axis=1) for q in range(Q)], axis=0))
        lhs[:R, :] = hi
        lhs[R:, :] = lo
        big = lax.dot_general(lhs[...], c_hi[...], nt, preferred_element_type=F32)
        part = big[:R] + big[R:] + lax.dot_general(lhs[:R], c_lo[...], nt, preferred_element_type=F32)
        for q in range(Q):
            for t in range(H):
                for v in range(W // 128):
                    image_out[H * q + t, 8 * v : 8 * v + 8, :] = part[
                        8 * q : 8 * q + 8, t * W + v * 128 : t * W + (v + 1) * 128
                    ]
        L = W // 128 * 8
        for j in range(B):
            image_out[j, L : L + 1, :] = curv
        sends(2, B, "base", lambda to: image_out.at[to, pl.ds(0, L + 1)], lambda to: image_in.at[b, pl.ds(0, L + 1)])
        image_in[b] = image_out[b]
        waits(recv, 2, image_in.at[pl.ds(0, B - 1), pl.ds(0, L + 1)])
        summed = image_in[0]
        for t in range(1, B):
            summed = summed + image_in[t]
        rest = pltpu.roll(row, 128 - R, 1) + pltpu.roll(summed[L : L + 1, :], 128 - 2 * R, 1)
        coef = coefficients(i == 0, row, rest, gamma_old, alpha_old)
        beta, alpha = coef[0][1], coef[0][2]
        for q in range(1, Q):
            beta = jnp.where(mine_q == q, coef[q][1], beta)
            alpha = jnp.where(mine_q == q, coef[q][2], alpha)
        r = resid[now, b]
        hess = h_ref[:, pl.ds(pl.multiple_of(mine_t * W, W), W)]
        image = jnp.concatenate([summed[8 * v : 8 * v + 8] for v in range(W // 128)], axis=1)
        w = image + hess * r + beta * w_own[...]
        w_own[...] = w
        resid[later, b] = r - alpha * w
        sends(3, B, "base", lambda to: resid.at[later, b], lambda to: resid.at[later, b])
        move(now, g, coef)
        waits(send, 2, image_out.at[pl.ds(0, B - 1), pl.ds(0, L + 1)])
        waits(recv, 3, resid.at[0, pl.ds(0, B - 1)])
        waits(send, 3, resid.at[0, pl.ds(0, B - 1)])
        return [c[0] for c in coef], [c[2] for c in coef]

    ones = [jnp.ones((8, 1), F32)] * Q
    gamma_old, alpha_old = lax.fori_loop(0, ITERS - 1, step, (ones, ones))

    now = (ITERS - 1) % 2
    g, row, curv = flows(now)
    image_out[0, 0:1, :] = curv
    image_in[b, 0:1, :] = curv
    sends(2, B, "base", lambda to: image_out.at[0, pl.ds(0, 1)], lambda to: image_in.at[b, pl.ds(0, 1)])
    waits(recv, 2, image_in.at[pl.ds(0, B - 1), pl.ds(0, 1)])
    rest = image_in[0, 0:1, :]
    for t in range(1, B):
        rest = rest + image_in[t, 0:1, :]
    rest = pltpu.roll(row, 128 - R, 1) + pltpu.roll(rest, 128 - 2 * R, 1)
    coef = coefficients(False, row, rest, gamma_old, alpha_old)
    move(now, g, coef)
    for k in range(K):
        y_ref[k] = gs_ref[k] * jnp.sqrt(w_ref[k : k + 1, :])
    waits(send, 2, image_out.at[pl.ds(0, B - 1), pl.ds(0, 1)])


def per_device(S, B, right_sides, base_hessian, sensitivity, weights, outage_factors, outaged):
    K, N, M = sensitivity.shape
    R = right_sides.shape[0]
    Q = R // 8
    H = B // Q
    W = N // H
    vmem = pl.BlockSpec(memory_space=pltpu.VMEM)
    tall = W // 128 * 8 + 8
    return pl.pallas_call(
        functools.partial(kernel, S, B),
        out_shape=(jax.ShapeDtypeStruct((R, N), F32), jax.ShapeDtypeStruct((K, R, M), F32)),
        in_specs=[vmem] * 5 + [pl.BlockSpec(memory_space=pltpu.SMEM)],
        out_specs=(vmem, vmem),
        scratch_shapes=[
            pltpu.VMEM((N, K * M), BF16),
            pltpu.VMEM((N, K * M), BF16),
            pltpu.VMEM((2 * R, max(N, K * M)), BF16),
            pltpu.VMEM((S, 8, 128), F32),
            pltpu.VMEM((S, 8, 128), F32),
            pltpu.VMEM((S, 16, 128), F32),
            pltpu.VMEM((B, tall, 128), F32),
            pltpu.VMEM((B, tall, 128), F32),
            pltpu.VMEM((2, B, 8, W), F32),
            pltpu.VMEM((B, 8, W), F32),
            pltpu.VMEM((8, W), F32),
            pltpu.VMEM((K, R, M), F32),
            pltpu.VMEM((K, R, M), F32),
            pltpu.SemaphoreType.DMA((4,)),
            pltpu.SemaphoreType.DMA((4,)),
        ],
        compiler_params=pltpu.CompilerParams(
            collective_id=0, has_side_effects=True, vmem_limit_bytes=32 * 1024 * 1024
        ),
    )(right_sides, base_hessian.reshape(1, N), sensitivity, weights, outage_factors, outaged)


def solution(mesh):
    placed = (
        P(None, "scen"),
        P("scen"),
        P("base", "scen", None),
        P("base", None),
        P("base", None),
        P("base"),
    )
    return jax.shard_map(
        functools.partial(per_device, mesh.shape["scen"], mesh.shape["base"]),
        mesh=mesh,
        in_specs=placed,
        out_specs=(P(None, "scen"), P("base", None, None)),
        check_vma=False,
    )
```

time: 273 us -> 99.7 us (0.37)
  blocking collectives: 191 us -> 0 us
  Pallas kernels: 0 us -> 92.8 us
  waiting for transfers between devices: 29.1 us -> 0 us
  starting transfers between devices: 20.3 us -> 0 us
  other arithmetic: 13 us -> 0 us
  matrix products: 10.5 us -> 0 us
    all_to_all x13 -> x0, blocking collectives: 191 us -> none  [sent_to_all(): lax.all_to_all(jnp.broadcast_to(value[None], (count, *value.shape)), axis...]
    pallas_call x0 -> x1, Pallas kernels: none -> 92.8 us  [per_device(): pl.pallas_call(functools.partial(kernel, S, B), out_shape=(jax.ShapeDtype...]
    all_to_all x3 -> x0, waiting for transfers between devices: 29.1 us -> none  [sent_to_all(): lax.all_to_all(jnp.broadcast_to(value[None], (count, *value.shape)), axis...]
    all_to_all x3 -> x0, starting transfers between devices: 20.3 us -> none  [sent_to_all(): lax.all_to_all(jnp.broadcast_to(value[None], (count, *value.shape)), axis...]
    dot_general x11 -> x0, matrix products: 10.5 us -> none  [the longest x5 5.38 us: per_device(): jnp.einsum('knm,krm->rn', sensitivity, apply_spread_back, precision=HIGHE...]
    reduce_sum x25 -> x0, other arithmetic: 8 us -> none  [the longest x16 5.43 us: taken_together(): return sent_to_all(value, axis).sum(axis=0)]
    broadcast_in_dim x16 -> x0, local copies, waits for them, and re-layouts: 6.63 us -> none  [sent_to_all(): jnp.broadcast_to(value[None], (count, *value.shape))]
    unnamed x19 -> x14, local copies, waits for them, and re-layouts: 0.35 us -> 6.02 us
  transfers between devices with their start and end apart: 3 -> 0, of which waited for: 3 -> 0; matrix products, arithmetic and copies ran while one was open for 1% -> 0% of each run, Pallas kernels for 0% -> 0%
where the time goes in v1:
time: 99.7 us; the launch traced here: 99.4 us
  Pallas kernels  92.8 us (93%)
  local copies, waits for them, and re-layouts  6.02 us (6%)
    pallas_call x1, Pallas kernels, per_device(): pl.pallas_call(functools.partial(kernel, S, B), out_shape=(jax.ShapeDtype...  92.8 us
    unnamed x14, local copies, waits for them, and re-layouts  6.02 us

profile of v1, /device:TPU:1, one launch (start us, length us, event | category | flops | bytes accessed | tf_op | source)
XLA Modules:
  0.0 99.4 jit_solution(8274103820257062563)
XLA Ops:
  0.6 0.0 copy-start.5
  0.6 0.6 copy-done.5
  1.3 0.0 copy-start
  1.3 1.2 %copy-done = f32[4,512,128]{2,1,0:T(8,128)S(1)} copy-done((f32[4,512,128]{2,1,0:T(8,128)S(1)}, f32[4,512,128]{2,1,0:T(8,128)}, u32[]{:S(2)}) %copy-start) | copy-done | bytes 1048600
  2.5 0.0 copy-start.1
  2.5 0.8 copy-done.1
  3.4 0.0 copy-start.2
  3.4 0.7 copy-done.2
  4.0 0.0 copy-start.3
  4.0 0.7 copy-done.3
  4.7 0.0 copy-start.4
  4.7 0.7 copy-done.4
  5.4 92.8 %shard_map.77 = (f32[32,512]{1,0:T(8,128)S(1)}, f32[4,32,128]{2,1,0:T(8,128)S(1)}) custom-call(f32[32,512]{1,0:T(8,128)S(1)} %copy-done.1, f32[1,512]{1,0:T(1,128)S(1)} %bitcast.1, f32[4,512,128]{2,1,0:T(8,128)S(1)} %copy-done, f32[4,128]{1,0:T(4,128)S(1)} %copy-done.3, f32[4,128]{1,0:T(4,128)S(1)} %copy-done.4, s32[4]{0:T(128)S(1)} %copy-done.5), custom_call_target="tpu_custom_call" | custom-call | tf_op jit(solution)/shard_map/pallas_call | solution.py:228
  98.2 0.6 copy.10
  98.8 0.6 copy.11
Async XLA Ops:
  0.6 0.7 copy-start.5
  1.3 1.2 %copy-start = (f32[4,512,128]{2,1,0:T(8,128)S(1)}, f32[4,512,128]{2,1,0:T(8,128)}, u32[]{:S(2)}) copy-start(f32[4,512,128]{2,1,0:T(8,128)} %a_ref.1) | copy-start | bytes 3145732
  2.5 0.8 copy-start.1
  3.4 0.7 copy-start.2
  4.0 0.7 copy-start.3
  4.7 0.7 copy-start.4
